TPU v7x, 128 devices: a whole 4x4x4 slice. The times are simulated.
128 devices in a mesh: gz: 2 (over x_hi), xy: 64 (over x_lo, y, z, core).
Axes of the slice: x: 4 (x_hi: 2, x_lo: 2; x = x_hi * 2 + x_lo), y: 4, z: 4, core: 2. Of those that a mesh axis runs over, the one named last changes fastest.
Arguments:
- section_image: bfloat16 [4, 256, 2048], P('gz', 'xy'), may hold values from -6 to 6
- crack_mask: int32 [4, 256, 2048], P('gz', 'xy'), may hold values 0 or 1
- fold_mask: int32 [4, 256, 2048], P('gz', 'xy'), may hold values 0 or 1
- first_weight: bfloat16 [9, 32], replicated, may hold values from -2 to 2
- first_bias: float32 [32], replicated, may hold values from -2 to 2
- second_weight: bfloat16 [9, 32, 32], replicated, may hold values from -0.5 to 0.5
- second_bias: float32 [32], replicated, may hold values from -2 to 2
- middle_weight: bfloat16 [27, 64, 32], replicated, may hold values from -0.3125 to 0.3125
- middle_bias: float32 [64], replicated, may hold values from -2 to 2
- deeper_weight: bfloat16 [27, 64, 64], replicated, may hold values from -0.21875 to 0.21875
- deeper_bias: float32 [64], replicated, may hold values from -2 to 2
- lift_weight: bfloat16 [32, 64], replicated, may hold values from -1 to 1
- lift_bias: float32 [32], replicated, may hold values from -2 to 2
- decode_weight: bfloat16 [9, 32, 32], replicated, may hold values from -0.5 to 0.5
- decode_bias: float32 [32], replicated, may hold values from -2 to 2
- head_weight: bfloat16 [3, 32], replicated, may hold values from -1.5 to 1.5
- head_bias: float32 [3], replicated, may hold values from -2 to 2
Outputs:
- affinity: float32 [3, 4, 2048, 256], P(None, 'gz', 'xy')
All inputs are finite; a program needn't handle non-finite values. No bound on the sum of `crack_mask` or of `fold_mask` on one device may be relied on, other than what follows from the above.
Results may differ from a plain program's by a relative error of at most 0.0055.
Values may be sent and summed in bfloat16 or wider, within the bound.
A program may use at most 128 MiB of HBM per device.

v0:
```python
import jax
import jax.numpy as jnp
from jax import lax
from jax.experimental import pallas as pl
from jax.experimental.pallas import tpu as pltpu
from jax.sharding import PartitionSpec as P

BF16 = jnp.bfloat16
F32 = jnp.float32
MESH = pl.DeviceIdType.MESH
CHIPS = 32


def exchange_kernel(image_ref, crack_ref, fold_ref, strip_ref, band, tile, strip, a_send, a_recv, b_send, b_recv):
    gz = lax.axis_index("gz")
    xy = lax.axis_index("xy")
    core = lax.rem(xy, 2)
    chip = lax.div(xy, 2)
    twin = xy + 1 - 2 * core
    close = ((1 - gz, xy), (gz, twin), (1 - gz, twin))
    far = [(gz, 2 * lax.rem(chip + k, CHIPS) + core) for k in range(1, CHIPS)]

    barrier = pltpu.get_barrier_semaphore()
    for device in (*close, *far):
        pl.semaphore_signal(barrier, inc=1, device_id=device, device_id_type=MESH)

    keep = ((1 - crack_ref[...]) * (1 - fold_ref[...])).astype(F32)
    gated = image_ref[...].astype(F32) * keep
    gated = jnp.concatenate([gated[0], gated[1]], axis=0)
    band[0] = jnp.concatenate([gated[:, :1024], gated[:, 1024:]], axis=0).astype(BF16)

    pl.semaphore_wait(barrier, len(close) + len(far))
    copies = []
    for k, device in enumerate(close):
        copy = pltpu.make_async_remote_copy(
            src_ref=band.at[0], dst_ref=band.at[k + 1], send_sem=a_send.at[k], recv_sem=a_recv.at[k],
            device_id=device, device_id_type=MESH,
        )
        copy.start()
        copies.append(copy)
    for copy in copies:
        copy.wait()

    sub = lax.broadcasted_iota(jnp.int32, (8, 128), 0)
    lane = lax.broadcasted_iota(jnp.int32, (8, 128), 1)
    shift = jnp.where(core == 0, 16, 112)
    own = (lane >= 16 - 16 * core) & (lane < 128 - 16 * core)
    left = lane < 64
    windows = []
    for group in range(2):
        parts = []
        for c in range(2):
            slot = jnp.where(group == gz, 0, 1) + jnp.where(c == core, 0, 2)
            parts.append(band[slot].astype(F32))
        tiles = ([], [])
        for k in range(16):
            rows = slice(8 * (k // 8), 8 * (k // 8) + 8)
            lanes = slice(128 * (k % 8), 128 * (k % 8) + 128)
            low, high = parts[0][rows, lanes], parts[1][rows, lanes]
            zero = jnp.where(sub < 4, low, pltpu.roll(high, 4, 0))
            one = jnp.where(sub < 4, pltpu.roll(low, 4, 0), high)
            tiles[0].append(pltpu.roll(zero, shift, 1))
            tiles[1].append(pltpu.roll(one, shift, 1))
        found = []
        for q in range(2):
            moved = []
            for k in range(16):
                beside = jnp.where(core == 0, tiles[q][(k - 1) % 16], tiles[q][(k + 1) % 16])
                moved.append(jnp.where(own, tiles[q][k], beside))
            found.append(moved)
        windows.append(found)
    for k in range(16):
        even, odd = [], []
        for group in range(2):
            zero, one = windows[group][0][k], windows[group][1][k]
            even.append(jnp.where(left, zero, pltpu.roll(one, 64, 1)))
            odd.append(jnp.where(left, pltpu.roll(zero, 64, 1), one))
        tile[2 * k] = jnp.concatenate(even, axis=0).astype(BF16)
        tile[2 * k + 1] = jnp.concatenate(odd, axis=0).astype(BF16)

    for device in far:
        copy = pltpu.make_async_remote_copy(
            src_ref=tile.at[lax.div(device[1], 2)], dst_ref=strip.at[chip], send_sem=b_send, recv_sem=b_recv,
            device_id=device, device_id_type=MESH,
        )
        copy.start()
    strip[chip] = tile[chip]
    others = pl.ds(0, CHIPS - 1)
    pltpu.make_async_copy(strip.at[others], strip.at[others], b_recv).wait()
    strip_ref[...] = strip[...]
    pltpu.make_async_copy(tile.at[others], tile.at[others], b_send).wait()


def exchange(image, crack, fold, own_barrier=True):
    params = dict(collective_id=0) if own_barrier else {}
    return pl.pallas_call(
        exchange_kernel,
        out_shape=jax.ShapeDtypeStruct((CHIPS, 16, 128), BF16),
        in_specs=[pl.BlockSpec(memory_space=pltpu.VMEM)] * 3,
        out_specs=pl.BlockSpec(memory_space=pltpu.VMEM),
        scratch_shapes=[
            pltpu.VMEM((4, 16, 1024), BF16),
            pltpu.VMEM((CHIPS, 16, 128), BF16),
            pltpu.VMEM((CHIPS, 16, 128), BF16),
            pltpu.SemaphoreType.DMA((3,)),
            pltpu.SemaphoreType.DMA((3,)),
            pltpu.SemaphoreType.DMA,
            pltpu.SemaphoreType.DMA,
        ],
        compiler_params=pltpu.CompilerParams(has_side_effects=True, **params),
        name="exchange",
    )(image, crack, fold)


def iota(shape, dim):
    return lax.broadcasted_iota(jnp.int32, shape, dim)


def dot(lhs, rhs):
    return jnp.dot(lhs, rhs, preferred_element_type=F32)


def column_of(row):
    n = row.shape[1]
    eye = iota((n, n), 0) == iota((n, n), 1)
    return jnp.sum(jnp.where(eye, row, 0.0), axis=1, keepdims=True)


def neighbours(field):
    lanes = field.shape[1]
    lane = iota(field.shape, 1)
    below = jnp.where(lane == 0, 0.0, pltpu.roll(field, 1, 1))
    above = jnp.where(lane == lanes - 1, 0.0, pltpu.roll(field, lanes - 1, 1))
    return below, field, above


def relu_plus(summed, offset, channels):
    rows, lanes = summed.shape
    parts = summed.reshape(rows // channels, channels, lanes) + offset[None]
    return jnp.maximum(parts, 0.0).reshape(rows, lanes)


def band(weight_ref, band_ref, tap, blocks, group, span):
    out_ch, in_ch = weight_ref.shape[1], weight_ref.shape[2]
    band_ref[...] = jnp.zeros_like(band_ref)
    for block in range(blocks):
        for a in range(3):
            piece = weight_ref[tap(block, a)]
            for m in range(group):
                start = block * span + (m + a) * in_ch
                band_ref[m * out_ch : (m + 1) * out_ch, start : start + in_ch] = piece


def network_kernel(
    strip_ref,
    w1_ref, b1_ref, w2_ref, b2_ref, wm_ref, bm_ref, wd_ref, bd_ref, wl_ref, bl_ref, wc_ref, bc_ref, wh_ref, bh_ref,
    out_ref,
    t1, t2, tm, td, tc, tl, th,
    vol, one, two, joined, pooled, mid, deep, dec, last,
):
    gz = lax.axis_index("gz")
    xy = lax.axis_index("xy")
    first = xy == 0
    final = xy == lax.axis_size("xy") - 1

    base = jnp.zeros((32, 256), F32)
    lane = iota((32, 256), 1)
    w1 = w1_ref[...].astype(F32)
    for a in range(3):
        for b in range(3):
            col = column_of(w1[3 * a + b : 3 * a + b + 1])
            base = jnp.where(lane == 64 * b + a, col, base)

    @pl.loop(0, 46)
    def _(i):
        t1[pl.ds(pl.multiple_of(i * 32, 32), 32), :] = pltpu.roll(base, i, 1).astype(BF16)

    band(w2_ref, t2, lambda block, a: 3 * a + block, 3, 4, 192)
    band(wc_ref, tc, lambda block, a: 3 * a + block, 3, 4, 192)

    def solid_tap(block, a):
        e, b = divmod(block, 3)
        e = jnp.where(gz == 0, e, 2 - e)
        return 9 * e + 3 * a + b

    band(wm_ref, tm, solid_tap, 9, 4, 192)
    band(wd_ref, td, solid_tap, 9, 2, 256)
    tl[...] = jnp.zeros_like(tl)
    for m in range(4):
        tl[32 * m : 32 * m + 32, 64 * m : 64 * m + 64] = wl_ref[...]
    th[...] = jnp.zeros_like(th)
    wh = wh_ref[...].astype(F32)
    row = iota((24, 256), 0)
    lane = iota((24, 256), 1)
    spread_h = jnp.zeros((24, 256), F32)
    pick = (iota((32, 256), 0) == lax.rem(iota((32, 256), 1), 32)).astype(BF16)
    wide = dot(wh_ref[...], pick)
    for k in range(3):
        here = (row // 8 == k) & (row % 8 == lane // 32)
        spread_h = jnp.where(here, wide[k : k + 1], spread_h)
    th[...] = spread_h.astype(BF16)

    b1 = column_of(b1_ref[...])
    b2 = column_of(b2_ref[...])
    bm = column_of(bm_ref[...])
    bd = column_of(bd_ref[...])
    bl = column_of(bl_ref[...])
    bc = column_of(bc_ref[...])
    hrow = iota((24, 1), 0)
    bh_row = bh_ref[...]
    bh = jnp.where(hrow < 8, bh_row[:, 0:1], jnp.where(hrow < 16, bh_row[:, 1:2], bh_row[:, 2:3]))

    strip = strip_ref[...].astype(F32).reshape(32, 2, 8, 128)
    u = iota((64, 128), 0)
    l = iota((64, 128), 1)
    place = 32 * xy - 8 + u
    inside = (u < 48) & (place >= 0) & (place < 32 * lax.axis_size("xy"))
    for s in range(4):
        rows = strip[:, s // 2].reshape(256, 128).astype(BF16)
        select = jnp.where(inside & (l == 64 * (s % 2) + 8 + u), 1.0, 0.0).astype(BF16)
        turned = lax.dot_general(select, rows, (((1,), (1,)), ((), ())), preferred_element_type=F32)
        t = jnp.where(gz == 0, s, 3 - s)
        for b, part in enumerate(neighbours(turned)):
            vol[t, 64 * b : 64 * b + 64, :] = part.astype(BF16)

    @pl.loop(0, 4)
    def _(t):
        field = vol[t]
        for chunk in range(2):
            rows = slice(736 * chunk, 736 * chunk + 736)
            found = relu_plus(dot(t1[rows, 0:192], field), b1, 32)
            for b, part in enumerate(neighbours(found)):
                one[t, b, rows, :] = part.astype(BF16)

    @pl.when(first)
    def _():
        one[:, :, 0 : 7 * 32, :] = jnp.zeros((4, 3, 7 * 32, 256), BF16)

    @pl.when(final)
    def _():
        one[:, :, 39 * 32 : 46 * 32, :] = jnp.zeros((4, 3, 7 * 32, 256), BF16)

    @pl.loop(0, 11)
    def _(g):
        start = pl.multiple_of(g * 128, 128)
        half = pl.multiple_of(g * 64, 64)
        for t in range(4):
            field = jnp.concatenate([one[t, b, pl.ds(start, 192), :] for b in range(3)], axis=0)
            found = relu_plus(dot(t2[...], field), b2, 32)
            if t < 2:
                two[t, pl.ds(start, 128), :] = found.astype(BF16)
            pairs = found.reshape(2, 2, 32, 256)
            pairs = jnp.maximum(pairs[:, 0], pairs[:, 1]).reshape(64, 256)
            pairs = jnp.maximum(pairs, pltpu.roll(pairs, 255, 1))
            joined[t, pl.ds(half, 64), :] = pairs.astype(BF16)

    fine = iota((256, 384), 0)
    coarse = iota((256, 384), 1)
    pick = jnp.where(fine == 2 * (coarse % 128 + coarse // 128 - 1), 1.0, 0.0).astype(BF16)
    pooled[:, :, 0:128] = jnp.zeros((3, 704, 128), BF16)
    for t in range(4):
        found = dot(joined[t], pick).astype(BF16)
        for b in range(3):
            pooled[b, :, 128 * (t + 1) : 128 * (t + 2)] = found[:, 128 * b : 128 * b + 128]

    @pl.when(first)
    def _():
        pooled[:, 0:96, :] = jnp.zeros((3, 96, 640), BF16)

    @pl.when(final)
    def _():
        pooled[:, 19 * 32 : 22 * 32, :] = jnp.zeros((3, 96, 640), BF16)

    mid[:, :, 0:128] = jnp.zeros((3, 1280, 128), BF16)

    @pl.loop(0, 5)
    def _(g):
        start = pl.multiple_of(g * 128, 128)
        field = jnp.concatenate(
            [pooled[b, pl.ds(start, 192), 128 * e : 128 * e + 384] for e in range(3) for b in range(3)], axis=0
        )
        found = relu_plus(dot(tm[...], field), bm, 64)
        rows = pl.ds(pl.multiple_of(g * 256, 256), 256)
        for t in range(3):
            for b, part in enumerate(neighbours(found[:, 128 * t : 128 * t + 128])):
                mid[b, rows, 128 * (t + 1) : 128 * (t + 2)] = part.astype(BF16)

    @pl.when(first)
    def _():
        mid[:, 0:128, :] = jnp.zeros((3, 128, 512), BF16)

    @pl.when(final)
    def _():
        mid[:, 18 * 64 : 20 * 64, :] = jnp.zeros((3, 128, 512), BF16)

    @pl.loop(0, 9)
    def _(g):
        start = pl.multiple_of(g * 128, 128)
        field = jnp.concatenate(
            [mid[b, pl.ds(start, 256), 128 * e : 128 * e + 256] for e in range(3) for b in range(3)], axis=0
        )
        deep[pl.ds(start, 128), :] = relu_plus(dot(td[...], field), bd, 64).astype(BF16)

    fine = iota((256, 256), 1)
    coarse = iota((256, 256), 0)
    double = jnp.where(fine // 2 == coarse % 128, 1.0, 0.0).astype(BF16)
    for g in range(5):
        count = 4 if g < 4 else 2
        rows = dot(tl[0 : 32 * count, 0 : 64 * count], deep[256 * g : 256 * g + 64 * count, :])
        rows = (rows.reshape(count, 32, 256) + bl[None]).reshape(32 * count, 256)
        high = rows.astype(BF16)
        low = (rows - high.astype(F32)).astype(BF16)
        for t in range(2):
            both = jnp.concatenate([high[:, 128 * t : 128 * t + 128], low[:, 128 * t : 128 * t + 128]], axis=1)
            lifted = dot(both, double)
            for r in range(count):
                for p in range(2):
                    v = 2 * (4 * g + r) + p
                    old = two[t, 32 * (v + 4) : 32 * (v + 5), :].astype(F32)
                    found = jnp.maximum(lifted[32 * r : 32 * r + 32] + old, 0.0)
                    for b, part in enumerate(neighbours(found)):
                        dec[t, b, 32 * v : 32 * v + 32, :] = part.astype(BF16)

    @pl.when(first)
    def _():
        dec[:, :, 0:64, :] = jnp.zeros((2, 3, 64, 256), BF16)

    @pl.when(final)
    def _():
        dec[:, :, 34 * 32 : 36 * 32, :] = jnp.zeros((2, 3, 64, 256), BF16)

    @pl.loop(0, 4)
    def _(g):
        for t in range(2):
            parts = []
            for h in range(2):
                start = pl.multiple_of(g * 256 + 128 * h + 32, 32)
                field = jnp.concatenate([dec[t, b, pl.ds(start, 192), :] for b in range(3)], axis=0)
                parts.append(relu_plus(dot(tc[...], field), bc, 32).astype(BF16))
            logits = dot(th[...], jnp.concatenate(parts, axis=0)) + bh
            found = jax.nn.sigmoid(logits)
            s = jnp.where(gz == 0, t, 1 - t)
            for k in range(3):
                out_ref[k, s, pl.ds(pl.multiple_of(g * 8, 8), 8), :] = found[8 * k : 8 * k + 8]


def network(strip, *weights):
    scratch = [
        pltpu.VMEM((1472, 256), BF16),
        pltpu.VMEM((128, 576), BF16),
        pltpu.VMEM((256, 1728), BF16),
        pltpu.VMEM((128, 2304), BF16),
        pltpu.VMEM((128, 576), BF16),
        pltpu.VMEM((128, 256), BF16),
        pltpu.VMEM((24, 256), BF16),
        pltpu.VMEM((4, 192, 256), BF16),
        pltpu.VMEM((4, 3, 1472, 256), BF16),
        pltpu.VMEM((2, 1408, 256), BF16),
        pltpu.VMEM((4, 704, 256), BF16),
        pltpu.VMEM((3, 704, 640), BF16),
        pltpu.VMEM((3, 1280, 512), BF16),
        pltpu.VMEM((1152, 256), BF16),
        pltpu.VMEM((2, 3, 1152, 256), BF16),
        pltpu.VMEM((1024, 256), BF16),
    ]
    return pl.pallas_call(
        network_kernel,
        out_shape=jax.ShapeDtypeStruct((3, 2, 32, 256), F32),
        in_specs=[pl.BlockSpec(memory_space=pltpu.VMEM)] * 15,
        out_specs=pl.BlockSpec(memory_space=pltpu.VMEM),
        scratch_shapes=scratch,
        compiler_params=pltpu.CompilerParams(vmem_limit_bytes=48 * 1024 * 1024),
        name="network",
    )(strip, *weights)


def body(image, crack, fold, *weights):
    rows = [weight[None] if weight.ndim == 1 else weight for weight in weights]
    strip = exchange(image, crack, fold)
    return network(strip.reshape(CHIPS * 16, 128), *rows)


def solution(mesh):
    in_specs = (P("gz", "xy", None),) * 3 + (P(),) * 14
    out_specs = P(None, "gz", "xy", None)
    return jax.shard_map(body, mesh=mesh, in_specs=in_specs, out_specs=out_specs, check_vma=False)
```

profile of v0, /device:TPU:1, one launch (start us, length us, event | category | flops | bytes accessed | tf_op | source)
XLA Modules:
  0.0 45.3 jit_solution(799959501070260593)
XLA Ops:
  0.0 18.6 %exchange.1 = bf16[32,16,128]{2,1,0:T(8,128)(2,1)} custom-call(bf16[2,4,2048]{2,1,0:T(4,128)(2,1)} %image_ref.1, s32[2,4,2048]{2,1,0:T(4,128)} %crack_ref.1, s32[2,4,2048]{2,1,0:T(4,128)} %fold_ref.1), custom_call_target="tpu_custom_call" | custom-call | tf_op jit(solution)/shard_map/exchange/pallas_call | solution.py:96
  18.7 0.0 copy-done.14
  18.7 0.0 copy-start
  18.7 0.0 copy-start.2
  18.7 0.0 copy-start.3
  18.7 0.0 copy-start.4
  18.7 0.0 copy-start.5
  18.7 0.0 copy-start.6
  18.7 0.0 copy-start.7
  18.8 0.0 copy-start.8
  18.8 0.0 copy-start.9
  18.8 0.0 copy-start.10
  18.8 0.0 copy-start.11
  18.8 0.0 copy-start.12
  18.8 0.0 copy-start.13
  18.8 0.3 copy.18.wm_ref
  19.1 0.0 copy-done.1
  19.1 0.5 %copy-done = bf16[32,16,128]{2,1,0:T(8,128)(2,1)S(1)} copy-done((bf16[32,16,128]{2,1,0:T(8,128)(2,1)S(1)}, bf16[32,16,128]{2,1,0:T(8,128)(2,1)}, u32[]{:S(2)}) %copy-start) | copy-done | bytes 131096
  19.6 0.0 copy-done.2
  19.6 0.0 copy-done.3
  19.7 0.0 copy-done.4
  19.7 0.0 copy-done.5
  19.7 0.0 copy-done.6
  19.7 25.5 %network.1 = f32[3,2,32,256]{3,2,1,0:T(8,128)} custom-call(bf16[512,128]{1,0:T(8,128)(2,1)S(1)} %bitcast.8, bf16[9,32]{1,0:T(8,128)(2,1)S(1)} %copy-done.5, f32[1,32]{1,0:T(1,128)S(1)} %bitcast.9, bf16[9,32,32]{2,1,0:T(8,128)(2,1)S(1)} %copy-done.2, f32[1,32]{1,0:T(1,128)S(1)} %bitcast.10, bf16[27,64,32]{2,1,0:T(8,128)(2,1)S(1)} %copy.18.wm_ref, ...), custom_call_target="tpu_custom_call" | custom-call | tf_op jit(solution)/shard_map/network/pallas_call | solution.py:366
  (9 shorter events, 0.0 us)
Async XLA Ops:
  0.0 18.7 %copy-start.14 = (bf16[27,64,32]{1,2,0:T(8,128)(2,1)S(1)}, bf16[27,64,32]{1,2,0:T(8,128)(2,1)}, u32[]{:S(2)}) copy-start(bf16[27,64,32]{1,2,0:T(8,128)(2,1)} %param.24) | copy-start | bytes 331780
  0.0 19.1 %copy-start.1 = (bf16[27,64,64]{2,1,0:T(8,128)(2,1)S(1)}, bf16[27,64,64]{2,1,0:T(8,128)(2,1)}, u32[]{:S(2)}) copy-start(bf16[27,64,64]{2,1,0:T(8,128)(2,1)} %wd_ref.1) | copy-start | bytes 663556
  18.7 0.9 %copy-start = (bf16[32,16,128]{2,1,0:T(8,128)(2,1)S(1)}, bf16[32,16,128]{2,1,0:T(8,128)(2,1)}, u32[]{:S(2)}) copy-start(bf16[32,16,128]{2,1,0:T(8,128)(2,1)} %exchange.1) | copy-start | bytes 393220
  18.7 0.9 %copy-start.2 = (bf16[9,32,32]{2,1,0:T(8,128)(2,1)S(1)}, bf16[9,32,32]{2,1,0:T(8,128)(2,1)}, u32[]{:S(2)}) copy-start(bf16[9,32,32]{2,1,0:T(8,128)(2,1)} %w2_ref.1) | copy-start | bytes 55300
  18.7 1.0 %copy-start.3 = (bf16[9,32,32]{2,1,0:T(8,128)(2,1)S(1)}, bf16[9,32,32]{2,1,0:T(8,128)(2,1)}, u32[]{:S(2)}) copy-start(bf16[9,32,32]{2,1,0:T(8,128)(2,1)} %wc_ref.1) | copy-start | bytes 55300
  18.7 1.0 %copy-start.4 = (bf16[32,64]{1,0:T(8,128)(2,1)S(1)}, bf16[32,64]{1,0:T(8,128)(2,1)}, u32[]{:S(2)}) copy-start(bf16[32,64]{1,0:T(8,128)(2,1)} %wl_ref.1) | copy-start | bytes 12292
  18.7 0.9 %copy-start.5 = (bf16[9,32]{1,0:T(8,128)(2,1)S(1)}, bf16[9,32]{1,0:T(8,128)(2,1)}, u32[]{:S(2)}) copy-start(bf16[9,32]{1,0:T(8,128)(2,1)} %w1_ref.1) | copy-start | bytes 1732
  18.7 0.9 %copy-start.6 = (bf16[3,32]{1,0:T(4,128)(2,1)S(1)}, bf16[3,32]{1,0:T(4,128)(2,1)}, u32[]{:S(2)}) copy-start(bf16[3,32]{1,0:T(4,128)(2,1)} %wh_ref.1) | copy-start | bytes 580
  18.7 0.9 %copy-start.7 = (f32[32]{0:T(128)S(1)}, f32[32]{0:T(128)}, u32[]{:S(2)}) copy-start(f32[32]{0:T(128)} %param.21) | copy-start | bytes 388
  18.8 0.9 %copy-start.8 = (f32[32]{0:T(128)S(1)}, f32[32]{0:T(128)}, u32[]{:S(2)}) copy-start(f32[32]{0:T(128)} %param.23) | copy-start | bytes 388
  18.8 0.9 %copy-start.9 = (f32[64]{0:T(128)S(1)}, f32[64]{0:T(128)}, u32[]{:S(2)}) copy-start(f32[64]{0:T(128)} %param.25) | copy-start | bytes 772
  18.8 0.9 %copy-start.10 = (f32[64]{0:T(128)S(1)}, f32[64]{0:T(128)}, u32[]{:S(2)}) copy-start(f32[64]{0:T(128)} %param.27) | copy-start | bytes 772
  18.8 0.9 %copy-start.11 = (f32[32]{0:T(128)S(1)}, f32[32]{0:T(128)}, u32[]{:S(2)}) copy-start(f32[32]{0:T(128)} %param.29) | copy-start | bytes 388
  18.8 0.9 %copy-start.12 = (f32[32]{0:T(128)S(1)}, f32[32]{0:T(128)}, u32[]{:S(2)}) copy-start(f32[32]{0:T(128)} %param.31) | copy-start | bytes 388
  18.8 0.9 %copy-start.13 = (f32[3]{0:T(128)S(1)}, f32[3]{0:T(128)}, u32[]{:S(2)}) copy-start(f32[3]{0:T(128)} %param.33) | copy-start | bytes 40
where the time goes:
time: 45.4 us; the launch traced here: 45.3 us
  Pallas kernels  44.2 us (97%)
  local copies, waits for them, and re-layouts  0.9 us (2%)
    pallas_call x1, Pallas kernels, network(): pl.pallas_call(network_kernel, out_shape=jax.ShapeDtypeStruct((3, 2, 32,...  25.5 us
    pallas_call x1, Pallas kernels, exchange(): pl.pallas_call(exchange_kernel, out_shape=jax.ShapeDtypeStruct((CHIPS, 16...  18.6 us

commit v1 on v0

--- a/solution.py
+++ b/solution.py
@@ -223,7 +223,7 @@
         for b, part in enumerate(neighbours(turned)):
             vol[t, 64 * b : 64 * b + 64, :] = part.astype(BF16)
 
-    @pl.loop(0, 4)
+    @pl.loop(0, 4, unroll=4)
     def _(t):
         field = vol[t]
         for chunk in range(2):
@@ -240,7 +240,7 @@
     def _():
         one[:, :, 39 * 32 : 46 * 32, :] = jnp.zeros((4, 3, 7 * 32, 256), BF16)
 
-    @pl.loop(0, 11)
+    @pl.loop(0, 11, unroll=11)
     def _(g):
         start = pl.multiple_of(g * 128, 128)
         half = pl.multiple_of(g * 64, 64)
@@ -273,7 +273,7 @@
 
     mid[:, :, 0:128] = jnp.zeros((3, 1280, 128), BF16)
 
-    @pl.loop(0, 5)
+    @pl.loop(0, 5, unroll=5)
     def _(g):
         start = pl.multiple_of(g * 128, 128)
         field = jnp.concatenate(
@@ -293,7 +293,7 @@
     def _():
         mid[:, 18 * 64 : 20 * 64, :] = jnp.zeros((3, 128, 512), BF16)
 
-    @pl.loop(0, 9)
+    @pl.loop(0, 9, unroll=9)
     def _(g):
         start = pl.multiple_of(g * 128, 128)
         field = jnp.concatenate(
@@ -329,7 +329,7 @@
     def _():
         dec[:, :, 34 * 32 : 36 * 32, :] = jnp.zeros((2, 3, 64, 256), BF16)
 
-    @pl.loop(0, 4)
+    @pl.loop(0, 4, unroll=4)
     def _(g):
         for t in range(2):
             parts = []

time: 45.4 us -> 39.2 us (0.86)
  Pallas kernels: 44.2 us -> 38 us
    pallas_call x1, Pallas kernels: 25.5 us -> 19.4 us  [network(): pl.pallas_call(network_kernel, out_shape=jax.ShapeDtypeStruct((3, 2, 32,...]
where the time goes in v1:
time: 39.2 us; the launch traced here: 39.1 us
  Pallas kernels  38 us (97%)
  local copies, waits for them, and re-layouts  0.9 us (2%)
    pallas_call x1, Pallas kernels, network(): pl.pallas_call(network_kernel, out_shape=jax.ShapeDtypeStruct((3, 2, 32,...  19.4 us
    pallas_call x1, Pallas kernels, exchange(): pl.pallas_call(exchange_kernel, out_shape=jax.ShapeDtypeStruct((CHIPS, 16...  18.6 us
    unnamed x31, local copies, waits for them, and re-layouts  0.9 us

profile of v1, /device:TPU:1, one launch (start us, length us, event | category | flops | bytes accessed | tf_op | source)
XLA Modules:
  0.0 39.1 jit_solution(5716107859614797182)
XLA Ops:
  0.0 18.6 %exchange.1 = bf16[32,16,128]{2,1,0:T(8,128)(2,1)} custom-call(bf16[2,4,2048]{2,1,0:T(4,128)(2,1)} %image_ref.1, s32[2,4,2048]{2,1,0:T(4,128)} %crack_ref.1, s32[2,4,2048]{2,1,0:T(4,128)} %fold_ref.1), custom_call_target="tpu_custom_call" | custom-call | tf_op jit(solution)/shard_map/exchange/pallas_call | solution.py:96
  18.7 0.0 copy-done.14
  18.7 0.0 copy-start
  18.7 0.0 copy-start.2
  18.7 0.0 copy-start.3
  18.7 0.0 copy-start.4
  18.7 0.0 copy-start.5
  18.7 0.0 copy-start.6
  18.7 0.0 copy-start.7
  18.8 0.0 copy-start.8
  18.8 0.0 copy-start.9
  18.8 0.0 copy-start.10
  18.8 0.0 copy-start.11
  18.8 0.0 copy-start.12
  18.8 0.0 copy-start.13
  18.8 0.3 copy.18.wm_ref
  19.1 0.0 copy-done.1
  19.1 0.5 %copy-done = bf16[32,16,128]{2,1,0:T(8,128)(2,1)S(1)} copy-done((bf16[32,16,128]{2,1,0:T(8,128)(2,1)S(1)}, bf16[32,16,128]{2,1,0:T(8,128)(2,1)}, u32[]{:S(2)}) %copy-start) | copy-done | bytes 131096
  19.6 0.0 copy-done.2
  19.6 0.0 copy-done.3
  19.7 0.0 copy-done.4
  19.7 0.0 copy-done.5
  19.7 0.0 copy-done.6
  19.7 19.4 %network.1 = f32[3,2,32,256]{3,2,1,0:T(8,128)} custom-call(bf16[512,128]{1,0:T(8,128)(2,1)S(1)} %bitcast.8, bf16[9,32]{1,0:T(8,128)(2,1)S(1)} %copy-done.5, f32[1,32]{1,0:T(1,128)S(1)} %bitcast.9, bf16[9,32,32]{2,1,0:T(8,128)(2,1)S(1)} %copy-done.2, f32[1,32]{1,0:T(1,128)S(1)} %bitcast.10, bf16[27,64,32]{2,1,0:T(8,128)(2,1)S(1)} %copy.18.wm_ref, ...), custom_call_target="tpu_custom_call" | custom-call | tf_op jit(solution)/shard_map/network/pallas_call | solution.py:366
  (9 shorter events, 0.0 us)
Async XLA Ops:
  0.0 18.7 %copy-start.14 = (bf16[27,64,32]{1,2,0:T(8,128)(2,1)S(1)}, bf16[27,64,32]{1,2,0:T(8,128)(2,1)}, u32[]{:S(2)}) copy-start(bf16[27,64,32]{1,2,0:T(8,128)(2,1)} %param.24) | copy-start | bytes 331780
  0.0 19.1 %copy-start.1 = (bf16[27,64,64]{2,1,0:T(8,128)(2,1)S(1)}, bf16[27,64,64]{2,1,0:T(8,128)(2,1)}, u32[]{:S(2)}) copy-start(bf16[27,64,64]{2,1,0:T(8,128)(2,1)} %wd_ref.1) | copy-start | bytes 663556
  18.7 0.9 %copy-start = (bf16[32,16,128]{2,1,0:T(8,128)(2,1)S(1)}, bf16[32,16,128]{2,1,0:T(8,128)(2,1)}, u32[]{:S(2)}) copy-start(bf16[32,16,128]{2,1,0:T(8,128)(2,1)} %exchange.1) | copy-start | bytes 393220
  18.7 0.9 %copy-start.2 = (bf16[9,32,32]{2,1,0:T(8,128)(2,1)S(1)}, bf16[9,32,32]{2,1,0:T(8,128)(2,1)}, u32[]{:S(2)}) copy-start(bf16[9,32,32]{2,1,0:T(8,128)(2,1)} %w2_ref.1) | copy-start | bytes 55300
  18.7 1.0 %copy-start.3 = (bf16[9,32,32]{2,1,0:T(8,128)(2,1)S(1)}, bf16[9,32,32]{2,1,0:T(8,128)(2,1)}, u32[]{:S(2)}) copy-start(bf16[9,32,32]{2,1,0:T(8,128)(2,1)} %wc_ref.1) | copy-start | bytes 55300
  18.7 1.0 %copy-start.4 = (bf16[32,64]{1,0:T(8,128)(2,1)S(1)}, bf16[32,64]{1,0:T(8,128)(2,1)}, u32[]{:S(2)}) copy-start(bf16[32,64]{1,0:T(8,128)(2,1)} %wl_ref.1) | copy-start | bytes 12292
  18.7 0.9 %copy-start.5 = (bf16[9,32]{1,0:T(8,128)(2,1)S(1)}, bf16[9,32]{1,0:T(8,128)(2,1)}, u32[]{:S(2)}) copy-start(bf16[9,32]{1,0:T(8,128)(2,1)} %w1_ref.1) | copy-start | bytes 1732
  18.7 0.9 %copy-start.6 = (bf16[3,32]{1,0:T(4,128)(2,1)S(1)}, bf16[3,32]{1,0:T(4,128)(2,1)}, u32[]{:S(2)}) copy-start(bf16[3,32]{1,0:T(4,128)(2,1)} %wh_ref.1) | copy-start | bytes 580
  18.7 0.9 %copy-start.7 = (f32[32]{0:T(128)S(1)}, f32[32]{0:T(128)}, u32[]{:S(2)}) copy-start(f32[32]{0:T(128)} %param.21) | copy-start | bytes 388
  18.8 0.9 %copy-start.8 = (f32[32]{0:T(128)S(1)}, f32[32]{0:T(128)}, u32[]{:S(2)}) copy-start(f32[32]{0:T(128)} %param.23) | copy-start | bytes 388
  18.8 0.9 %copy-start.9 = (f32[64]{0:T(128)S(1)}, f32[64]{0:T(128)}, u32[]{:S(2)}) copy-start(f32[64]{0:T(128)} %param.25) | copy-start | bytes 772
  18.8 0.9 %copy-start.10 = (f32[64]{0:T(128)S(1)}, f32[64]{0:T(128)}, u32[]{:S(2)}) copy-start(f32[64]{0:T(128)} %param.27) | copy-start | bytes 772
  18.8 0.9 %copy-start.11 = (f32[32]{0:T(128)S(1)}, f32[32]{0:T(128)}, u32[]{:S(2)}) copy-start(f32[32]{0:T(128)} %param.29) | copy-start | bytes 388
  18.8 0.9 %copy-start.12 = (f32[32]{0:T(128)S(1)}, f32[32]{0:T(128)}, u32[]{:S(2)}) copy-start(f32[32]{0:T(128)} %param.31) | copy-start | bytes 388
  18.8 0.9 %copy-start.13 = (f32[3]{0:T(128)S(1)}, f32[3]{0:T(128)}, u32[]{:S(2)}) copy-start(f32[3]{0:T(128)} %param.33) | copy-start | bytes 40
